TPU v7x, 32 devices: a whole 2x2x4 slice. The times are simulated.
32 devices in a mesh: groups: 2 (over x), ctx: 16 (over z, y, core).
Axes of the slice: x: 2, y: 2, z: 4, core: 2. Of those that a mesh axis runs over, the one named last changes fastest.
Arguments:
- hidden: bfloat16 [4096, 4096], P(('groups', 'ctx')), parts along dimension 0, may hold values from -6 to 6
- frozen_query: bfloat16 [4096, 2048], P(('groups', 'ctx')), parts along dimension 0, may hold values from -18 to 18
- frozen_key: bfloat16 [4096, 512], P(('groups', 'ctx')), parts along dimension 0, may hold values from -18 to 18
- frozen_value: bfloat16 [4096, 512], P(('groups', 'ctx')), parts along dimension 0, may hold values from -6 to 6
- adapter_bank: bfloat16 [16, 64, 21504], P('ctx'), may hold values from -0.57 to 0.57
- request_shards: int32 [6], P('groups'), parts along dimension 0, may hold values from 1 to 9, 16 in all
- request_adapter: int32 [6], P('groups'), parts along dimension 0, may hold values from 0 to 15
- adapter_owner: int32 [16], replicated, may hold values from 0 to 15, each once
Outputs:
- attention: bfloat16 [4096, 2048], P(('groups', 'ctx')), parts along dimension 0
- adapter_output: bfloat16 [4096, 4096], P(('groups', 'ctx')), parts along dimension 0
There are 2 independent parts, one for each index of `groups`. A program takes and returns all parts, laid end to end along the dimension named above; an argument that names none is the same for every part. Nothing has to cross between parts.
Inputs may be any that keep to these rules, and one draw needn't show every extreme that they name: `request_shards`: request lengths sum to 16; the longest has exactly 9 shards. `adapter_owner`: a permutation: every bank entry holds exactly one adapter.
All inputs are finite; a program needn't handle non-finite values.
Results may differ from a plain program's by a relative error of at most 0.012.
Values may be sent and summed in bfloat16 or wider, within the bound.
No kernel may reach another device: no remote copies, remote signals or barrier semaphores. Data moves between devices by JAX's collectives and lax.ppermute only.
A program may use at most 64 MiB of HBM per device.

v0:
```python
import functools

import jax
import jax.numpy as jnp
from jax import lax
from jax.experimental import pallas as pl
from jax.experimental.pallas import tpu as pltpu
from jax.sharding import PartitionSpec as P

HEAD_SIZE = 128
QUERY_HEADS = 16
KEY_VALUE_HEADS = 4
GROUP_SPLIT = QUERY_HEADS // KEY_VALUE_HEADS

adapter_scale = 0.5
rope_theta = 500000.0
score_masked = -1e30

VMEM_LIMIT = 24 * 1024 * 1024

ROW_BLOCKS = 4
CHUNKS = 8


def rope_tables(positions):
    half_dim = HEAD_SIZE // 2
    frequency = rope_theta ** (-(jnp.arange(half_dim, dtype=jnp.float32) * 2.0) / HEAD_SIZE)
    angles = positions.astype(jnp.float32)[..., None] * frequency
    cosines = jnp.cos(angles)
    sines = jnp.sin(angles)
    return (jnp.concatenate([cosines, cosines], -1), jnp.concatenate([-sines, sines], -1))


class Parts:
    def __init__(self, model_width, query_width, key_width):
        d, q, k = model_width, query_width, key_width
        up = 3 * d
        self.kv = ((d, d // CHUNKS), (2 * d, d // CHUNKS), (up + q, 2 * k // CHUNKS))
        self.q = ((0, d // CHUNKS), (up, q // CHUNKS))
        self.o = ((up + q + 2 * k, q // CHUNKS), (up + 2 * q + 2 * k, d // CHUNKS))
        self.all = self.kv + self.q + self.o
        self.widths = tuple(sum(w for _, w in part) for part in (self.kv, self.q, self.o))


def vmem(count=1):
    return [pl.BlockSpec(memory_space=pltpu.VMEM)] * count


def smem(count=1):
    return [pl.BlockSpec(memory_space=pltpu.SMEM)] * count


PARAMS = pltpu.CompilerParams(vmem_limit_bytes=VMEM_LIMIT)


OWN_INDEX, OWN_HALF, COUNT, ENTRY = 0, 1, 2, 8


def layout(lengths_ref, which, shards):
    starts, start, length = [jnp.int32(0)], jnp.int32(0), lengths_ref[which, 0]
    for r in range(1, lengths_ref.shape[1]):
        starts.append(starts[-1] + lengths_ref[which, r - 1])
        longer = lengths_ref[which, r] > length
        start = jnp.where(longer, starts[-1], start)
        length = jnp.where(longer, lengths_ref[which, r], length)
    return starts, start + lax.div(length, 2)


def plan_kernel(shards, reach, me_ref, lengths_ref, adapters_ref, owner_ref, out_ref):
    own_index, own_half = me_ref[0], me_ref[1]
    starts, offset = layout(lengths_ref, 0, shards)
    own_packed = lax.rem(own_index + offset, shards)
    first = jnp.int32(0)
    for start in starts[1:]:
        first = jnp.where(start <= own_packed, start, first)
    out_ref[OWN_INDEX] = own_index
    out_ref[OWN_HALF] = own_half
    out_ref[COUNT] = jnp.minimum(own_packed - first, reach) + 1
    for which in range(lengths_ref.shape[0]):
        starts, offset = layout(lengths_ref, which, shards)
        entries = [owner_ref[adapters_ref[which, r]] for r in range(len(starts))]
        at = ENTRY + shards * (own_half if which == 0 else 1 - own_half)
        for shard in range(shards):
            packed = lax.rem(shard + offset, shards)
            entry = entries[0]
            for start, later in zip(starts[1:], entries[1:]):
                entry = jnp.where(start <= packed, later, entry)
            out_ref[at + shard] = entry


def make_plan(shards, reach, me, lengths, adapters, owner):
    return pl.pallas_call(
        functools.partial(plan_kernel, shards, reach),
        out_shape=jax.ShapeDtypeStruct((ENTRY + lengths.shape[0] * shards,), jnp.int32),
        in_specs=smem(4),
        out_specs=smem()[0],
        name="plan",
    )(me, lengths, adapters, owner)


def pack_kernel(parts, halves, x_ref, bank_ref, out):
    own_half = x_ref[1]
    for block in range(out.shape[0]):
        piece = block % (ROW_BLOCKS * CHUNKS // halves)
        rows = pl.ds((piece % ROW_BLOCKS) * 16, 16)
        chunk = (piece // ROW_BLOCKS) * halves + own_half
        at = 0
        for first, width in parts.all:
            start = pl.multiple_of(first + chunk * width, 128)
            out[block, :, at : at + width] = bank_ref[0, rows, pl.ds(start, width)]
            at += width


def pack(parts, halves, shards, me, bank):
    width = sum(parts.widths)
    return pl.pallas_call(
        functools.partial(pack_kernel, parts, halves),
        out_shape=jax.ShapeDtypeStruct((shards, 16, width), bank.dtype),
        in_specs=smem() + vmem(),
        out_specs=vmem()[0],
        compiler_params=PARAMS,
        name="pack",
    )(me, bank)


ROUTE_STEPS = 4


def route_kernel(plan_ref, spread_ref, out_ref):
    for i in range(out_ref.shape[0]):
        dest = pl.program_id(0) * out_ref.shape[0] + i
        out_ref[i] = spread_ref[plan_ref[ENTRY + dest]]


def route(plan, spread):
    dests = plan.shape[0] - ENTRY
    return pl.pallas_call(
        route_kernel,
        out_shape=jax.ShapeDtypeStruct((dests,) + spread.shape[1:], spread.dtype),
        grid=(ROUTE_STEPS,),
        in_specs=smem() + vmem(),
        out_specs=pl.BlockSpec((dests // ROUTE_STEPS,) + spread.shape[1:], lambda i: (i, 0, 0)),
        compiler_params=PARAMS,
        name="route",
    )(plan, spread)


def factor(piece_ref, chunk, at, width):
    halves = piece_ref.shape[0]
    place = chunk // halves * ROW_BLOCKS
    rows = piece_ref[chunk % halves, place : place + ROW_BLOCKS, :, at : at + width]
    return rows.reshape(ROW_BLOCKS * 16, width)


def columns(chunk, width):
    return slice(chunk * width, (chunk + 1) * width)


def dot_nt(a, b):
    return lax.dot_general(a, b, (((1,), (1,)), ((), ())), preferred_element_type=jnp.float32)


def turn(x, cosines, sines):
    return x * cosines + pltpu.roll(x, HEAD_SIZE // 2, 1) * sines


def kv_kernel(plan_ref, hidden_ref, key_ref, value_ref, cos_ref, sin_ref, piece_ref, out_ref):
    d = hidden_ref.shape[1] // CHUNKS
    rank = ROW_BLOCKS * 16
    low = jnp.zeros((hidden_ref.shape[0], 2 * rank), jnp.float32)
    for chunk in range(CHUNKS):
        down = jnp.concatenate(
            [factor(piece_ref, chunk, 0, d), factor(piece_ref, chunk, d, d)], axis=0
        )
        low += dot_nt(hidden_ref[:, columns(chunk, d)], down)
    low = low.astype(jnp.bfloat16)
    width = 2 * key_ref.shape[1] // CHUNKS
    own = plan_ref[COUNT] - 1
    cosines, sines = cos_ref[own], sin_ref[own]
    for chunk in range(CHUNKS):
        is_key = chunk < CHUNKS // 2
        up = factor(piece_ref, chunk, 2 * d, width)
        part = low[:, :rank] if is_key else low[:, rank:]
        update = jnp.dot(part, up, preferred_element_type=jnp.float32)
        frozen = (key_ref if is_key else value_ref)[:, columns(chunk % (CHUNKS // 2), width)]
        result = frozen.astype(jnp.float32) + adapter_scale * update
        if is_key:
            result = turn(result, cosines, sines)
        out_ref[:, columns(chunk, width)] = result.astype(jnp.bfloat16)


def make_keys_values(plan, hidden, key, value, tables, pieces):
    return pl.pallas_call(
        kv_kernel,
        out_shape=jax.ShapeDtypeStruct((key.shape[0], 2 * key.shape[1]), jnp.bfloat16),
        in_specs=smem() + vmem(6),
        out_specs=vmem()[0],
        compiler_params=PARAMS,
        cost_estimate=pl.CostEstimate(
            flops=150_000_000, bytes_accessed=3 << 20, transcendentals=0
        ),
        name="keys_values",
    )(plan, hidden, key, value, *tables, pieces)


def query_kernel(at, plan_ref, hidden_ref, query_ref, cos_ref, sin_ref, piece_ref, out_ref):
    tokens = query_ref.shape[0]
    d = hidden_ref.shape[1] // CHUNKS
    width = query_ref.shape[1] // CHUNKS
    low = jnp.zeros((tokens, ROW_BLOCKS * 16), jnp.float32)
    for chunk in range(CHUNKS):
        low += dot_nt(hidden_ref[:, columns(chunk, d)], factor(piece_ref, chunk, at, d))
    low = low.astype(jnp.bfloat16)
    own = plan_ref[COUNT] - 1
    cosines, sines = cos_ref[own], sin_ref[own]
    for chunk in range(CHUNKS):
        up = factor(piece_ref, chunk, at + d, width)
        update = jnp.dot(low, up, preferred_element_type=jnp.float32)
        result = query_ref[:, columns(chunk, width)].astype(jnp.float32) + adapter_scale * update
        for part in range(width // HEAD_SIZE):
            head = chunk * (width // HEAD_SIZE) + part
            turned = turn(result[:, columns(part, HEAD_SIZE)], cosines, sines)
            out_ref[head // GROUP_SPLIT, pl.ds((head % GROUP_SPLIT) * tokens, tokens)] = (
                turned.astype(jnp.bfloat16)
            )


def make_queries(plan, hidden, query, tables, pieces, at):
    tokens = hidden.shape[0]
    return pl.pallas_call(
        functools.partial(query_kernel, at),
        out_shape=jax.ShapeDtypeStruct(
            (KEY_VALUE_HEADS, GROUP_SPLIT * tokens, HEAD_SIZE), jnp.bfloat16
        ),
        in_specs=smem() + vmem(5),
        out_specs=vmem()[0],
        compiler_params=PARAMS,
        cost_estimate=pl.CostEstimate(
            flops=100_000_000, bytes_accessed=3 << 20, transcendentals=0
        ),
        name="queries",
    )(plan, hidden, query, *tables, pieces)


REGION = 4


def attend_kernel(plan_ref, queries, *refs):
    blocks, (out_ref, high, acc) = refs[:-3], refs[-3:]
    count = plan_ref[COUNT]
    tokens = out_ref.shape[0]
    rows = GROUP_SPLIT * tokens
    bf16 = jnp.bfloat16
    base2 = 1.4426950408889634 / (HEAD_SIZE**0.5)
    ones = jnp.ones((tokens, HEAD_SIZE), bf16)

    def region(first, number):
        shards = blocks[first : first + number]
        for g in range(KEY_VALUE_HEADS):
            keys = [b[:, columns(g, HEAD_SIZE)] for b in shards]
            values = [
                jnp.concatenate([b[:, columns(KEY_VALUE_HEADS + g, HEAD_SIZE)], ones], axis=1)
                for b in shards
            ]
            score = dot_nt(queries[g], jnp.concatenate(keys, axis=0))
            tiles = [score[:, columns(i, tokens)] for i in range(number)]
            if first == 0:
                row = lax.broadcasted_iota(jnp.int32, (rows, tokens), 0) % tokens
                column = lax.broadcasted_iota(jnp.int32, (rows, tokens), 1)
                tiles = [jnp.where(column <= row, tiles[0], score_masked)]
            else:
                tiles = tiles[:1] + [
                    jnp.where(count > first + i, tiles[i], score_masked)
                    for i in range(1, number)
                ]
            top = functools.reduce(jnp.maximum, tiles)
            top = jnp.max(top, axis=1, keepdims=True) * base2
            top = jnp.broadcast_to(top, (rows, HEAD_SIZE))
            if first:
                old = high[g]
                top = jnp.maximum(old, top)
            weight = [jnp.exp2(t * base2 - top).astype(bf16) for t in tiles]
            blend = jnp.dot(
                jnp.concatenate(weight, axis=1),
                jnp.concatenate(values, axis=0),
                preferred_element_type=jnp.float32,
            )
            if first:
                shrink = jnp.exp2(old - top)
                blend += acc[g] * jnp.concatenate([shrink, shrink], axis=1)
            high[g] = top
            acc[g] = blend

    region(0, 1)
    for first in range(1, len(blocks), REGION):
        number = min(REGION, len(blocks) - first)
        pl.when(count > first)(functools.partial(region, first, number))

    for g in range(KEY_VALUE_HEADS):
        result = (acc[g, :, :HEAD_SIZE] / acc[g, :, HEAD_SIZE:]).astype(bf16)
        for j in range(GROUP_SPLIT):
            out_ref[:, columns(g * GROUP_SPLIT + j, HEAD_SIZE)] = result[columns(j, tokens)]


def attend(plan, queries, blocks):
    tokens = blocks[0].shape[0]
    rows = GROUP_SPLIT * tokens
    limit = VMEM_LIMIT if len(blocks) < 16 else 2 * VMEM_LIMIT
    return pl.pallas_call(
        attend_kernel,
        out_shape=jax.ShapeDtypeStruct((tokens, QUERY_HEADS * HEAD_SIZE), jnp.bfloat16),
        in_specs=smem() + vmem(1 + len(blocks)),
        out_specs=vmem()[0],
        scratch_shapes=[
            pltpu.VMEM((KEY_VALUE_HEADS, rows, HEAD_SIZE), jnp.float32),
            pltpu.VMEM((KEY_VALUE_HEADS, rows, 2 * HEAD_SIZE), jnp.float32),
        ],
        compiler_params=pltpu.CompilerParams(vmem_limit_bytes=limit),
        cost_estimate=pl.CostEstimate(
            flops=2_000_000_000, bytes_accessed=8 << 20, transcendentals=4 << 20
        ),
        name="attend",
    )(plan, queries, *blocks)


def output_kernel(at, attended_ref, piece_ref, out_ref):
    q_head = attended_ref.shape[1] // CHUNKS
    d = out_ref.shape[1] // CHUNKS
    low = jnp.zeros((attended_ref.shape[0], ROW_BLOCKS * 16), jnp.float32)
    for chunk in range(CHUNKS):
        down = factor(piece_ref, chunk, at, q_head)
        low += dot_nt(attended_ref[:, columns(chunk, q_head)], down)
    low = low.astype(jnp.bfloat16)
    for chunk in range(CHUNKS):
        result = adapter_scale * jnp.dot(
            low, factor(piece_ref, chunk, at + q_head, d), preferred_element_type=jnp.float32
        )
        out_ref[:, columns(chunk, d)] = result.astype(jnp.bfloat16)


def output_adapter(attended, pieces, model_width, at):
    return pl.pallas_call(
        functools.partial(output_kernel, at),
        out_shape=jax.ShapeDtypeStruct((attended.shape[0], model_width), jnp.bfloat16),
        in_specs=vmem(2),
        out_specs=vmem()[0],
        compiler_params=PARAMS,
        cost_estimate=pl.CostEstimate(
            flops=100_000_000, bytes_accessed=3 << 20, transcendentals=0
        ),
        name="output",
    )(attended, pieces)


def reach_pairs(shards, shift):
    longest = shards // 2 + 1
    low = -(longest // 2)
    runs = (
        [i % shards for i in range(low, low + longest)],
        [i % shards for i in range(low + longest, low + shards)],
    )
    limits = (longest, shards - longest - 1)
    return [
        (run[i], run[i + shift])
        for run, limit in zip(runs, limits)
        if shift < limit
        for i in range(len(run) - shift)
    ]


def body(
    hidden,
    frozen_query,
    frozen_key,
    frozen_value,
    adapter_bank,
    request_shards,
    request_adapter,
    adapter_owner,
):
    shards = lax.axis_size("ctx")
    groups = lax.axis_size("groups")
    tokens, model_width = hidden.shape
    halves = 2 if groups == 2 and 2 * shards == ROW_BLOCKS * CHUNKS else 1
    own_half = lax.axis_index("groups") if halves == 2 else 0
    me = jnp.stack([lax.axis_index("ctx"), own_half]).astype(jnp.int32)
    parts = Parts(model_width, frozen_query.shape[1], frozen_key.shape[1])
    reach = shards // 2

    packed = pack(parts, halves, shards, me, adapter_bank)
    spread = lax.all_to_all(packed, "ctx", split_axis=0, concat_axis=0, tiled=True)

    tables = rope_tables(jnp.arange((reach + 1) * tokens, dtype=jnp.int32).reshape(-1, tokens))
    requests = jnp.stack([request_shards, request_adapter])[:, None]
    if halves == 2:
        theirs = lax.ppermute(requests, "groups", [(0, 1), (1, 0)])
        requests = jnp.concatenate([requests, theirs], axis=1)
    plan = make_plan(shards, reach, me, requests[0], requests[1], adapter_owner)
    spread, tables = lax.optimization_barrier((spread, tables))

    def collect(pieces):
        axes = ("groups", "ctx") if halves == 2 else "ctx"
        pieces = lax.all_to_all(pieces, axes, split_axis=0, concat_axis=0, tiled=True)
        return pieces.reshape((halves, shards) + pieces.shape[1:])[:, : ROW_BLOCKS * CHUNKS]

    kv_width, q_width, _ = parts.widths
    pieces = collect(route(plan, spread))
    kv = make_keys_values(plan, hidden, frozen_key, frozen_value, tables, pieces)
    blocks = [kv] + [
        lax.ppermute(kv, "ctx", reach_pairs(shards, shift)) for shift in range(1, reach + 1)
    ]
    queries = make_queries(plan, hidden, frozen_query, tables, pieces, kv_width)
    attended = attend(plan, queries, blocks)
    return attended, output_adapter(attended, pieces, model_width, kv_width + q_width)


def solution(mesh):
    return jax.shard_map(
        body,
        mesh=mesh,
        in_specs=(
            P(("groups", "ctx"), None),
            P(("groups", "ctx"), None),
            P(("groups", "ctx"), None),
            P(("groups", "ctx"), None),
            P("ctx", None, None),
            P("groups"),
            P("groups"),
            P(),
        ),
        out_specs=(P(("groups", "ctx"), None), P(("groups", "ctx"), None)),
        check_vma=False,
    )
```

profile of v0, /device:TPU:0, one launch (start us, length us, event | category | flops | bytes accessed | tf_op | source)
XLA Modules:
  0.0 159.8 jit_solution(10257793814939755689)
XLA Ops:
  0.7 1.8 %copy-done.1 = bf16[1,64,21504]{2,1,0:T(8,128)(2,1)S(1)} copy-done((bf16[1,64,21504]{2,1,0:T(8,128)(2,1)S(1)}, bf16[1,64,21504]{2,1,0:T(8,128)(2,1)}, u32[]{:S(2)}) %copy-start.1) | copy-done | bytes 2752536
  2.5 1.8 %pack.1 = bf16[16,16,2688]{2,1,0:T(8,128)(2,1)} custom-call(s32[2]{0:T(128)S(1)} %pad_add_fusion.1.me_ref.x_ref, bf16[1,64,21504]{2,1,0:T(8,128)(2,1)S(1)} %copy-done.1), custom_call_target="tpu_custom_call" | custom-call | tf_op jit(solution)/shard_map/pack/pallas_call | solution.py:116
  4.3 7.4 %all-to-all-start = ((bf16[16,16,2688]{2,1,0:T(8,128)(2,1)}), bf16[16,16,2688]{2,1,0:T(8,128)(2,1)S(1)}, u32[]{:S(2)}, u32[]{:S(2)}) async-start(bf16[16,16,2688]{2,1,0:T(8,128)(2,1)} %pack.1), calls=%async_computation | async-start | bytes 2752512 | tf_op jit(solution)/shard_map/all_to_all | solution.py:391
  11.7 1.6 collective-permute-start
  13.3 2.1 %fusion = (f32[9,128,64]{2,1,0:T(8,128)S(1)}, f32[9,128,64]{2,1,0:T(8,128)S(1)}, f32[9,128,64]{2,1,0:T(8,128)S(1)}) fusion(f32[64]{0:T(128)S(1)} %multiply_power_fusion, f32[9,128]{1,0:T(8,128)S(1)} %add_convert_fusion), kind=kLoop, calls=%fused_computation.4 | loop fusion | flops 147456 | bytes 889600 | tf_op jit(solution)/shard_map/neg | solution.py:31
  16.4 1.4 plan.1.plan_ref
  17.8 22.4 %all-to-all-done.spread_ref = bf16[16,16,2688]{2,1,0:T(8,128)(2,1)S(1)} async-done(((bf16[16,16,2688]{2,1,0:T(8,128)(2,1)}), bf16[16,16,2688]{2,1,0:T(8,128)(2,1)S(1)}, u32[]{:S(2)}, u32[]{:S(2)}) %all-to-all-start) | async-done | bytes 1376288 | tf_op jit(solution)/shard_map/all_to_all | solution.py:391
  40.8 0.8 route.1
  41.7 71.7 %all_to_all.10 = bf16[32,16,2688]{2,1,0:T(8,128)(2,1)S(1)} all-to-all(bf16[32,16,2688]{2,1,0:T(8,128)(2,1)S(1)} %route.1), channel_id=1, replica_groups=mesh['groups'=2,'ctx'=16] {'groups','ctx'}, dimensions={0} | all-to-all | bytes 5505024 | tf_op jit(solution)/shard_map/all_to_all | solution.py:403
  113.4 1.3 keys_values.1.refs_0_
  114.7 0.7 collective-permute-start.8
  115.4 0.7 collective-permute-start.7
  117.5 4.8 %collective-permute-start.4 = (bf16[128,1024]{1,0:T(8,128)(2,1)S(1)}, bf16[128,1024]{1,0:T(8,128)(2,1)S(1)}, u32[]{:S(2)}, u32[]{:S(2)}) collective-permute-start(bf16[128,1024]{1,0:T(8,128)(2,1)S(1)} %keys_values.1.refs_0_), channel_id=1, source_target_pairs={{12,0},{13,1},{14,2},{15,3},{0,4},{5,9},{6,10},{7,11},{28,16},{29,... | collective-permute-start | bytes 786440 | tf_op jit(solution)/shard_map/ppermute | solution.py:410
  122.3 1.9 %collective-permute-start.3 = (bf16[128,1024]{1,0:T(8,128)(2,1)S(1)}, bf16[128,1024]{1,0:T(8,128)(2,1)S(1)}, u32[]{:S(2)}, u32[]{:S(2)}) collective-permute-start(bf16[128,1024]{1,0:T(8,128)(2,1)S(1)} %keys_values.1.refs_0_), channel_id=1, source_target_pairs={{12,15},{13,0},{14,1},{15,2},{0,3},{1,4},{5,8},{6,9},{7,10},{8,11}... | collective-permute-start | bytes 786440 | tf_op jit(solution)/shard_map/ppermute | solution.py:410
  124.2 1.9 %collective-permute-start.2 = (bf16[128,1024]{1,0:T(8,128)(2,1)S(1)}, bf16[128,1024]{1,0:T(8,128)(2,1)S(1)}, u32[]{:S(2)}, u32[]{:S(2)}) collective-permute-start(bf16[128,1024]{1,0:T(8,128)(2,1)S(1)} %keys_values.1.refs_0_), channel_id=1, source_target_pairs={{12,14},{13,15},{14,0},{15,1},{0,2},{1,3},{2,4},{5,7},{6,8},{7,9},... | collective-permute-start | bytes 786440 | tf_op jit(solution)/shard_map/ppermute | solution.py:410
  126.1 10.3 %collective-permute-start.1 = (bf16[128,1024]{1,0:T(8,128)(2,1)S(1)}, bf16[128,1024]{1,0:T(8,128)(2,1)S(1)}, u32[]{:S(2)}, u32[]{:S(2)}) collective-permute-start(bf16[128,1024]{1,0:T(8,128)(2,1)S(1)} %keys_values.1.refs_0_), channel_id=1, source_target_pairs={{12,13},{13,14},{14,15},{15,0},{0,1},{1,2},{2,3},{3,4},{5,6},{6,7}... | collective-permute-start | bytes 786440 | tf_op jit(solution)/shard_map/ppermute | solution.py:410
  136.4 1.5 queries.1
  137.9 10.4 %collective-permute-done.4.refs_4_ = bf16[128,1024]{1,0:T(8,128)(2,1)S(1)} collective-permute-done((bf16[128,1024]{1,0:T(8,128)(2,1)S(1)}, bf16[128,1024]{1,0:T(8,128)(2,1)S(1)}, u32[]{:S(2)}, u32[]{:S(2)}) %collective-permute-start.4) | collective-permute-done | bytes 262176 | tf_op jit(solution)/shard_map/ppermute | solution.py:410
  148.4 0.7 collective-permute-done.3.refs_3_
  149.0 2.8 %collective-permute-done.2.refs_2_ = bf16[128,1024]{1,0:T(8,128)(2,1)S(1)} collective-permute-done((bf16[128,1024]{1,0:T(8,128)(2,1)S(1)}, bf16[128,1024]{1,0:T(8,128)(2,1)S(1)}, u32[]{:S(2)}, u32[]{:S(2)}) %collective-permute-start.2) | collective-permute-done | bytes 262176 | tf_op jit(solution)/shard_map/ppermute | solution.py:410
  151.8 0.7 collective-permute-done.1.refs_1_
  152.5 4.4 %attend.1.attended_ref = bf16[128,2048]{1,0:T(8,128)(2,1)} custom-call(s32[40]{0:T(128)S(1)} %copy-done.6, bf16[4,512,128]{2,1,0:T(8,128)(2,1)S(1)} %queries.1, bf16[128,1024]{1,0:T(8,128)(2,1)S(1)} %keys_values.1.refs_0_, bf16[128,1024]{1,0:T(8,128)(2,1)S(1)} %collective-permute-done.1.refs_1_, bf16[128,1024]{1,0:T(8,128)(2,1)S(1)} %collective-permute-done.2.refs_2_, ...), custom_call_target="tpu_custom_call" | custom-call | flops 2000000000 | bytes 8388608 | tf_op jit(solution)/shard_map/attend/pallas_call | solution.py:309
  156.9 1.0 copy-done.3
  157.9 1.9 %output.1 = bf16[128,4096]{1,0:T(8,128)(2,1)} custom-call(bf16[128,2048]{1,0:T(8,128)(2,1)S(1)} %copy-done.3, bf16[2,16,16,2688]{3,2,1,0:T(8,128)(2,1)S(1)} %bitcast.11), custom_call_target="tpu_custom_call" | custom-call | flops 100000000 | bytes 3145728 | tf_op jit(solution)/shard_map/output/pallas_call | solution.py:342
  (31 shorter events, 3.1 us)
Async XLA Ops:
  0.7 1.8 %copy-start.1 = (bf16[1,64,21504]{2,1,0:T(8,128)(2,1)S(1)}, bf16[1,64,21504]{2,1,0:T(8,128)(2,1)}, u32[]{:S(2)}) copy-start(bf16[1,64,21504]{2,1,0:T(8,128)(2,1)} %bank_ref.1) | copy-start | bytes 8257540
  2.5 1.8 %copy-start.7 = (s32[2]{0:T(128)}, s32[2]{0:T(128)S(1)}, u32[]{:S(2)}) copy-start(s32[2]{0:T(128)S(1)} %pad_add_fusion.1.me_ref.x_ref) | copy-start | bytes 28
  2.5 9.2 %copy-start.8 = (s32[3]{0:T(128)S(1)}, s32[3]{0:T(128)}, u32[]{:S(2)}) copy-start(s32[3]{0:T(128)} %param.14) | copy-start | bytes 40
  2.5 9.2 %copy-start.9 = (s32[3]{0:T(128)S(1)}, s32[3]{0:T(128)}, u32[]{:S(2)}) copy-start(s32[3]{0:T(128)} %param.13) | copy-start | bytes 40
  4.3 35.9 %all-to-all-start = ((bf16[16,16,2688]{2,1,0:T(8,128)(2,1)}), bf16[16,16,2688]{2,1,0:T(8,128)(2,1)S(1)}, u32[]{:S(2)}, u32[]{:S(2)}) async-start(bf16[16,16,2688]{2,1,0:T(8,128)(2,1)} %pack.1), calls=%async_computation | async-start | bytes 2752512 | tf_op jit(solution)/shard_map/all_to_all | solution.py:391
  11.7 4.1 %collective-permute-start = (s32[2,1,3]{2,0,1:T(2,128)S(1)}, s32[2,1,3]{2,0,1:T(2,128)S(1)}, u32[]{:S(2)}, u32[]{:S(2)}) collective-permute-start(s32[2,1,3]{2,0,1:T(2,128)S(1)} %add_bitcast_fusion), channel_id=1, source_target_pairs={{0,16},{16,0},{1,17},{17,1},{2,18},{18,2},{3,19},{19,3},{4,20},{20... | collective-permute-start | bytes 80 | tf_op jit(solution)/shard_map/ppermute | solution.py:396
  40.2 0.6 copy-start.6
  41.7 71.7 %copy-start = (bf16[128,4096]{1,0:T(8,128)(2,1)S(1)}, bf16[128,4096]{1,0:T(8,128)(2,1)}, u32[]{:S(2)}) copy-start(bf16[128,4096]{1,0:T(8,128)(2,1)} %hidden_ref.3) | copy-start | bytes 3145732
  41.7 71.7 %copy-start.4 = (bf16[128,512]{1,0:T(8,128)(2,1)S(1)}, bf16[128,512]{1,0:T(8,128)(2,1)}, u32[]{:S(2)}) copy-start(bf16[128,512]{1,0:T(8,128)(2,1)} %key_ref.1) | copy-start | bytes 393220
  41.7 71.7 %copy-start.5 = (bf16[128,512]{1,0:T(8,128)(2,1)S(1)}, bf16[128,512]{1,0:T(8,128)(2,1)}, u32[]{:S(2)}) copy-start(bf16[128,512]{1,0:T(8,128)(2,1)} %value_ref.1) | copy-start | bytes 393220
  113.4 23.0 %copy-start.2 = (bf16[128,2048]{1,0:T(8,128)(2,1)S(1)}, bf16[128,2048]{1,0:T(8,128)(2,1)}, u32[]{:S(2)}) copy-start(bf16[128,2048]{1,0:T(8,128)(2,1)} %query_ref.1) | copy-start | bytes 1572868
  114.7 7.5 %collective-permute-start.8 = (bf16[128,1024]{1,0:T(8,128)(2,1)S(1)}, bf16[128,1024]{1,0:T(8,128)(2,1)S(1)}, u32[]{:S(2)}, u32[]{:S(2)}) collective-permute-start(bf16[128,1024]{1,0:T(8,128)(2,1)S(1)} %keys_values.1.refs_0_), channel_id=1, source_target_pairs={{12,4},{28,20}} | collective-permute-start | bytes 786440 | tf_op jit(solution)/shard_map/ppermute | solution.py:410
  115.4 8.8 %collective-permute-start.7 = (bf16[128,1024]{1,0:T(8,128)(2,1)S(1)}, bf16[128,1024]{1,0:T(8,128)(2,1)S(1)}, u32[]{:S(2)}, u32[]{:S(2)}) collective-permute-start(bf16[128,1024]{1,0:T(8,128)(2,1)S(1)} %keys_values.1.refs_0_), channel_id=1, source_target_pairs={{12,3},{13,4},{28,19},{29,20}} | collective-permute-start | bytes 786440 | tf_op jit(solution)/shard_map/ppermute | solution.py:410
  116.1 10.0 %collective-permute-start.6 = (bf16[128,1024]{1,0:T(8,128)(2,1)S(1)}, bf16[128,1024]{1,0:T(8,128)(2,1)S(1)}, u32[]{:S(2)}, u32[]{:S(2)}) collective-permute-start(bf16[128,1024]{1,0:T(8,128)(2,1)S(1)} %keys_values.1.refs_0_), channel_id=1, source_target_pairs={{12,2},{13,3},{14,4},{28,18},{29,19},{30,20}} | collective-permute-start | bytes 786440 | tf_op jit(solution)/shard_map/ppermute | solution.py:410
  116.8 21.1 %collective-permute-start.5 = (bf16[128,1024]{1,0:T(8,128)(2,1)S(1)}, bf16[128,1024]{1,0:T(8,128)(2,1)S(1)}, u32[]{:S(2)}, u32[]{:S(2)}) collective-permute-start(bf16[128,1024]{1,0:T(8,128)(2,1)S(1)} %keys_values.1.refs_0_), channel_id=1, source_target_pairs={{12,1},{13,2},{14,3},{15,4},{5,10},{6,11},{28,17},{29,18},{30,19},... | collective-permute-start | bytes 786440 | tf_op jit(solution)/shard_map/ppermute | solution.py:410
  117.5 30.9 %collective-permute-start.4 = (bf16[128,1024]{1,0:T(8,128)(2,1)S(1)}, bf16[128,1024]{1,0:T(8,128)(2,1)S(1)}, u32[]{:S(2)}, u32[]{:S(2)}) collective-permute-start(bf16[128,1024]{1,0:T(8,128)(2,1)S(1)} %keys_values.1.refs_0_), channel_id=1, source_target_pairs={{12,0},{13,1},{14,2},{15,3},{0,4},{5,9},{6,10},{7,11},{28,16},{29,... | collective-permute-start | bytes 786440 | tf_op jit(solution)/shard_map/ppermute | solution.py:410
  122.3 26.8 %collective-permute-start.3 = (bf16[128,1024]{1,0:T(8,128)(2,1)S(1)}, bf16[128,1024]{1,0:T(8,128)(2,1)S(1)}, u32[]{:S(2)}, u32[]{:S(2)}) collective-permute-start(bf16[128,1024]{1,0:T(8,128)(2,1)S(1)} %keys_values.1.refs_0_), channel_id=1, source_target_pairs={{12,15},{13,0},{14,1},{15,2},{0,3},{1,4},{5,8},{6,9},{7,10},{8,11}... | collective-permute-start | bytes 786440 | tf_op jit(solution)/shard_map/ppermute | solution.py:410
  124.2 27.6 %collective-permute-start.2 = (bf16[128,1024]{1,0:T(8,128)(2,1)S(1)}, bf16[128,1024]{1,0:T(8,128)(2,1)S(1)}, u32[]{:S(2)}, u32[]{:S(2)}) collective-permute-start(bf16[128,1024]{1,0:T(8,128)(2,1)S(1)} %keys_values.1.refs_0_), channel_id=1, source_target_pairs={{12,14},{13,15},{14,0},{15,1},{0,2},{1,3},{2,4},{5,7},{6,8},{7,9},... | collective-permute-start | bytes 786440 | tf_op jit(solution)/shard_map/ppermute | solution.py:410
  126.1 26.4 %collective-permute-start.1 = (bf16[128,1024]{1,0:T(8,128)(2,1)S(1)}, bf16[128,1024]{1,0:T(8,128)(2,1)S(1)}, u32[]{:S(2)}, u32[]{:S(2)}) collective-permute-start(bf16[128,1024]{1,0:T(8,128)(2,1)S(1)} %keys_values.1.refs_0_), channel_id=1, source_target_pairs={{12,13},{13,14},{14,15},{15,0},{0,1},{1,2},{2,3},{3,4},{5,6},{6,7}... | collective-permute-start | bytes 786440 | tf_op jit(solution)/shard_map/ppermute | solution.py:410
  156.9 1.0 copy-start.3
where the time goes:
time: 160 us
  blocking collectives  71.7 us (45%)
  waiting for transfers between devices  37 us (23%)
  starting transfers between devices  30.5 us (19%)
  Pallas kernels  13.1 us (8%)
  local copies, waits for them, and re-layouts  3.49 us (2%)
  other arithmetic  3.18 us (2%)
    all_to_all x1, blocking collectives, collect(): lax.all_to_all(pieces, axes, split_axis=0, concat_axis=0, tiled=True)  71.7 us
    all_to_all x1, waiting for transfers between devices, body(): lax.all_to_all(packed, 'ctx', split_axis=0, concat_axis=0, tiled=True)  22.4 us
    ppermute x8, starting transfers between devices, body(): lax.ppermute(kv, 'ctx', reach_pairs(shards, shift))  21.6 us
    ppermute x8, waiting for transfers between devices, body(): lax.ppermute(kv, 'ctx', reach_pairs(shards, shift))  14.6 us
    all_to_all x1, starting transfers between devices, body(): lax.all_to_all(packed, 'ctx', split_axis=0, concat_axis=0, tiled=True)  7.39 us
    pallas_call x1, Pallas kernels, attend(): pl.pallas_call(attend_kernel, out_shape=jax.ShapeDtypeStruct((tokens, QUE...  4.39 us
    unnamed x20, local copies, waits for them, and re-layouts  3.49 us
  transfers between devices with their start and end apart: 10, of which 5 were waited for; matrix products, arithmetic and copies ran while one was open for 2% of the time, Pallas kernels for 2%

commit v1 on v0

--- a/solution.py
+++ b/solution.py
@@ -126,20 +126,27 @@
 ROUTE_STEPS = 4
 
 
-def route_kernel(plan_ref, spread_ref, out_ref):
-    for i in range(out_ref.shape[0]):
-        dest = pl.program_id(0) * out_ref.shape[0] + i
-        out_ref[i] = spread_ref[plan_ref[ENTRY + dest]]
-
-
-def route(plan, spread):
+def route_kernel(plan_ref, spread_ref, *outs):
+    number = outs[0].shape[0]
+    for i in range(number):
+        entry = plan_ref[ENTRY + pl.program_id(0) * number + i]
+        at = 0
+        for out in outs:
+            out[i] = spread_ref[entry, :, at : at + out.shape[2]]
+            at += out.shape[2]
+
+
+def route(plan, spread, first_width):
     dests = plan.shape[0] - ENTRY
+    widths = (first_width, spread.shape[2] - first_width)
     return pl.pallas_call(
         route_kernel,
-        out_shape=jax.ShapeDtypeStruct((dests,) + spread.shape[1:], spread.dtype),
+        out_shape=[jax.ShapeDtypeStruct((dests, 16, w), spread.dtype) for w in widths],
         grid=(ROUTE_STEPS,),
         in_specs=smem() + vmem(),
-        out_specs=pl.BlockSpec((dests // ROUTE_STEPS,) + spread.shape[1:], lambda i: (i, 0, 0)),
+        out_specs=[
+            pl.BlockSpec((dests // ROUTE_STEPS, 16, w), lambda i: (i, 0, 0)) for w in widths
+        ],
         compiler_params=PARAMS,
         name="route",
     )(plan, spread)
@@ -242,12 +249,15 @@
     )(plan, hidden, query, *tables, pieces)
 
 
-REGION = 4
-
-
-def attend_kernel(plan_ref, queries, *refs):
-    blocks, (out_ref, high, acc) = refs[:-3], refs[-3:]
+REGION = 5
+
+
+def attend_kernel(steps, plan_ref, queries, *refs):
+    blocks, (out_ref, copy_ref, high, acc) = refs[:-4], refs[-4:]
     count = plan_ref[COUNT]
+    odd = lax.rem(plan_ref[OWN_INDEX], 2)
+    aside = 2 * odd - 1
+    steps = [s if even else s + aside for s, even in steps]
     tokens = out_ref.shape[0]
     rows = GROUP_SPLIT * tokens
     bf16 = jnp.bfloat16
@@ -269,9 +279,9 @@
                 column = lax.broadcasted_iota(jnp.int32, (rows, tokens), 1)
                 tiles = [jnp.where(column <= row, tiles[0], score_masked)]
             else:
-                tiles = tiles[:1] + [
-                    jnp.where(count > first + i, tiles[i], score_masked)
-                    for i in range(1, number)
+                tiles = [
+                    jnp.where((step > 0) & (step < count), tile, score_masked)
+                    for step, tile in zip(steps[first : first + number], tiles)
                 ]
             top = functools.reduce(jnp.maximum, tiles)
             top = jnp.max(top, axis=1, keepdims=True) * base2
@@ -294,23 +304,25 @@
     region(0, 1)
     for first in range(1, len(blocks), REGION):
         number = min(REGION, len(blocks) - first)
-        pl.when(count > first)(functools.partial(region, first, number))
+        nearest = functools.reduce(jnp.minimum, steps[first : first + number])
+        pl.when(count > nearest)(functools.partial(region, first, number))
 
     for g in range(KEY_VALUE_HEADS):
         result = (acc[g, :, :HEAD_SIZE] / acc[g, :, HEAD_SIZE:]).astype(bf16)
         for j in range(GROUP_SPLIT):
-            out_ref[:, columns(g * GROUP_SPLIT + j, HEAD_SIZE)] = result[columns(j, tokens)]
-
-
-def attend(plan, queries, blocks):
+            for ref in (out_ref, copy_ref):
+                ref[:, columns(g * GROUP_SPLIT + j, HEAD_SIZE)] = result[columns(j, tokens)]
+
+
+def attend(plan, queries, blocks, steps):
     tokens = blocks[0].shape[0]
     rows = GROUP_SPLIT * tokens
     limit = VMEM_LIMIT if len(blocks) < 16 else 2 * VMEM_LIMIT
     return pl.pallas_call(
-        attend_kernel,
-        out_shape=jax.ShapeDtypeStruct((tokens, QUERY_HEADS * HEAD_SIZE), jnp.bfloat16),
+        functools.partial(attend_kernel, steps),
+        out_shape=[jax.ShapeDtypeStruct((tokens, QUERY_HEADS * HEAD_SIZE), jnp.bfloat16)] * 2,
         in_specs=smem() + vmem(1 + len(blocks)),
-        out_specs=vmem()[0],
+        out_specs=vmem(2),
         scratch_shapes=[
             pltpu.VMEM((KEY_VALUE_HEADS, rows, HEAD_SIZE), jnp.float32),
             pltpu.VMEM((KEY_VALUE_HEADS, rows, 2 * HEAD_SIZE), jnp.float32),
@@ -352,7 +364,7 @@
     )(attended, pieces)
 
 
-def reach_pairs(shards, shift):
+def earlier_shards(shards):
     longest = shards // 2 + 1
     low = -(longest // 2)
     runs = (
@@ -360,12 +372,36 @@
         [i % shards for i in range(low + longest, low + shards)],
     )
     limits = (longest, shards - longest - 1)
-    return [
-        (run[i], run[i + shift])
-        for run, limit in zip(runs, limits)
-        if shift < limit
-        for i in range(len(run) - shift)
-    ]
+    earlier = {}
+    for run, limit in zip(runs, limits):
+        for i, shard in enumerate(run):
+            earlier[shard] = set(run[max(0, i - limit + 1) : i])
+    return earlier
+
+
+def shift_pairs(shards, shift):
+    earlier = earlier_shards(shards)
+    pairs = [((d - shift) % shards, d) for d in range(shards)]
+    return [(s, d) for s, d in pairs if s in earlier[d] or s in earlier[d ^ 1]]
+
+
+def swap_pairs(shards, shift):
+    earlier = earlier_shards(shards)
+    return [(d, d ^ 1) for d in range(shards) if (d - shift) % shards in earlier[d ^ 1]]
+
+
+def exchange(kv, shards, reach):
+    shifts = range(0, reach + 1, 2)
+    got = [kv] + [lax.ppermute(kv, "ctx", shift_pairs(shards, s)) for s in shifts[1:]]
+    swapped = [lax.ppermute(b, "ctx", swap_pairs(shards, s)) for s, b in zip(shifts, got)]
+    blocks, steps = [kv], [(0, True)]
+    for s, even, odd in zip(shifts, got, swapped):
+        if s:
+            blocks.append(even)
+            steps.append((s, True))
+        blocks.append(odd)
+        steps.append((s, False))
+    return blocks, steps
 
 
 def body(
@@ -404,14 +440,15 @@
         return pieces.reshape((halves, shards) + pieces.shape[1:])[:, : ROW_BLOCKS * CHUNKS]
 
     kv_width, q_width, _ = parts.widths
-    pieces = collect(route(plan, spread))
+    first, later = route(plan, spread, kv_width + q_width)
+    pieces = collect(first)
     kv = make_keys_values(plan, hidden, frozen_key, frozen_value, tables, pieces)
-    blocks = [kv] + [
-        lax.ppermute(kv, "ctx", reach_pairs(shards, shift)) for shift in range(1, reach + 1)
-    ]
+    blocks, steps = exchange(kv, shards, reach)
+    blocks[1], later = lax.optimization_barrier((blocks[1], later))
+    later = collect(later)
     queries = make_queries(plan, hidden, frozen_query, tables, pieces, kv_width)
-    attended = attend(plan, queries, blocks)
-    return attended, output_adapter(attended, pieces, model_width, kv_width + q_width)
+    attended, copy = attend(plan, queries, blocks, steps)
+    return attended, output_adapter(copy, later, model_width, 0)
 
 
 def solution(mesh):

time: 160 us -> 159 us (level)
  blocking collectives: 71.7 us -> 54.8 us
  waiting for transfers between devices: 37 us -> 51 us
  starting transfers between devices: 30.5 us -> 27.2 us
  local copies, waits for them, and re-layouts: 3.49 us -> 6.25 us
  Pallas kernels: 13.1 us -> 15 us
    all_to_all x1, blocking collectives: 71.7 us -> 54.8 us  [collect(): lax.all_to_all(pieces, axes, split_axis=0, concat_axis=0, tiled=True)]
    ppermute x8 -> x9, waiting for transfers between devices: 14.6 us -> 28.5 us  [the longest x4 27.4 us: exchange(): lax.ppermute(kv, 'ctx', shift_pairs(shards, s))]
    ppermute x8 -> x9, starting transfers between devices: 21.6 us -> 14.8 us  [the longest x4 8.03 us: exchange(): lax.ppermute(kv, 'ctx', shift_pairs(shards, s))]
    all_to_all x0 -> x1, starting transfers between devices: none -> 3.35 us  [collect(): lax.all_to_all(pieces, axes, split_axis=0, concat_axis=0, tiled=True)]
    unnamed x20 -> x28, local copies, waits for them, and re-layouts: 3.49 us -> 6.25 us
  transfers between devices with their start and end apart: 10 -> 12, of which waited for: 5 -> 4; matrix products, arithmetic and copies ran while one was open for 2% -> 2% of each run, Pallas kernels for 2% -> 5%
where the time goes in v1:
time: 159 us; the launch traced here: 158 us
  blocking collectives  54.8 us (34%)
  waiting for transfers between devices  51 us (32%)
  starting transfers between devices  27.2 us (17%)
  Pallas kernels  15 us (9%)
  local copies, waits for them, and re-layouts  6.25 us (4%)
  other arithmetic  3.18 us (2%)
    all_to_all x1, blocking collectives, collect(): lax.all_to_all(pieces, axes, split_axis=0, concat_axis=0, tiled=True)  54.8 us
    ppermute x4, waiting for transfers between devices, exchange(): lax.ppermute(kv, 'ctx', shift_pairs(shards, s))  27.4 us
    all_to_all x1, waiting for transfers between devices, body(): lax.all_to_all(packed, 'ctx', split_axis=0, concat_axis=0, tiled=True)  22.4 us
    ppermute x4, starting transfers between devices, exchange(): lax.ppermute(kv, 'ctx', shift_pairs(shards, s))  8.03 us
    all_to_all x1, starting transfers between devices, body(): lax.all_to_all(packed, 'ctx', split_axis=0, concat_axis=0, tiled=True)  7.52 us
    ppermute x5, starting transfers between devices, exchange(): lax.ppermute(b, 'ctx', swap_pairs(shards, s))  6.73 us
    unnamed x28, local copies, waits for them, and re-layouts  6.25 us
    pallas_call x1, Pallas kernels, attend(): pl.pallas_call(functools.partial(attend_kernel, steps), out_shape=[jax.Sh...  5.17 us
  transfers between devices with their start and end apart: 12, of which 4 were waited for; matrix products, arithmetic and copies ran while one was open for 2% of the time, Pallas kernels for 5%

profile of v1, /device:TPU:0, one launch (start us, length us, event | category | flops | bytes accessed | tf_op | source)
XLA Modules:
  0.0 158.3 jit_solution(3574152496575464210)
XLA Ops:
  0.7 1.8 %copy-done.2 = bf16[1,64,21504]{2,1,0:T(8,128)(2,1)S(1)} copy-done((bf16[1,64,21504]{2,1,0:T(8,128)(2,1)S(1)}, bf16[1,64,21504]{2,1,0:T(8,128)(2,1)}, u32[]{:S(2)}) %copy-start.2) | copy-done | bytes 2752536
  2.5 1.8 %pack.1 = bf16[16,16,2688]{2,1,0:T(8,128)(2,1)} custom-call(s32[2]{0:T(128)S(1)} %pad_add_fusion.1.me_ref.x_ref, bf16[1,64,21504]{2,1,0:T(8,128)(2,1)S(1)} %copy-done.2), custom_call_target="tpu_custom_call" | custom-call | tf_op jit(solution)/shard_map/pack/pallas_call | solution.py:116
  4.3 7.5 %all-to-all-start = ((bf16[16,16,2688]{2,1,0:T(8,128)(2,1)}), bf16[16,16,2688]{2,1,0:T(8,128)(2,1)S(1)}, u32[]{:S(2)}, u32[]{:S(2)}) async-start(bf16[16,16,2688]{2,1,0:T(8,128)(2,1)} %pack.1), calls=%async_computation | async-start | bytes 2752512 | tf_op jit(solution)/shard_map/all_to_all | solution.py:427
  11.8 1.6 collective-permute-start
  13.4 2.1 %fusion = (f32[9,128,64]{2,1,0:T(8,128)S(1)}, f32[9,128,64]{2,1,0:T(8,128)S(1)}, f32[9,128,64]{2,1,0:T(8,128)S(1)}) fusion(f32[64]{0:T(128)S(1)} %multiply_power_fusion, f32[9,128]{1,0:T(8,128)S(1)} %add_convert_fusion), kind=kLoop, calls=%fused_computation.4 | loop fusion | flops 147456 | bytes 889600 | tf_op jit(solution)/shard_map/neg | solution.py:31
  16.5 1.4 plan.1.plan_ref
  17.9 22.4 %all-to-all-done.spread_ref = bf16[16,16,2688]{2,1,0:T(8,128)(2,1)S(1)} async-done(((bf16[16,16,2688]{2,1,0:T(8,128)(2,1)}), bf16[16,16,2688]{2,1,0:T(8,128)(2,1)S(1)}, u32[]{:S(2)}, u32[]{:S(2)}) %all-to-all-start) | async-done | bytes 1376288 | tf_op jit(solution)/shard_map/all_to_all | solution.py:427
  41.8 0.9 copy-done.3
  42.7 54.8 %all_to_all.15 = bf16[32,16,1920]{2,1,0:T(8,128)(2,1)S(1)} all-to-all(bf16[32,16,1920]{2,1,0:T(8,128)(2,1)S(1)} %get-tuple-element.14), channel_id=1, replica_groups=mesh['groups'=2,'ctx'=16] {'groups','ctx'}, dimensions={0} | all-to-all | bytes 3932160 | tf_op jit(solution)/shard_map/all_to_all | solution.py:439
  97.5 1.3 keys_values.1.refs_0_
  98.8 1.6 collective-permute-start.1
  100.4 1.1 collective-permute-done.1.refs_1_
  102.2 3.4 %all-to-all-start.2 = ((bf16[32,16,768]{2,1,0:T(8,128)(2,1)}), bf16[32,16,768]{2,1,0:T(8,128)(2,1)}, u32[]{:S(2)}, u32[]{:S(2)}) async-start(bf16[32,16,768]{2,1,0:T(8,128)(2,1)} %copy-done.3), calls=%async_computation.2 | async-start | bytes 1572864 | tf_op jit(solution)/shard_map/all_to_all | solution.py:439
  107.0 4.8 %collective-permute-start.4 = (bf16[128,1024]{1,0:T(8,128)(2,1)S(1)}, bf16[128,1024]{1,0:T(8,128)(2,1)S(1)}, u32[]{:S(2)}, u32[]{:S(2)}) collective-permute-start(bf16[128,1024]{1,0:T(8,128)(2,1)S(1)} %keys_values.1.refs_0_), channel_id=1, source_target_pairs={{12,0},{13,1},{14,2},{15,3},{0,4},{1,5},{5,9},{6,10},{7,11},{28,16... | collective-permute-start | bytes 786440 | tf_op jit(solution)/shard_map/ppermute | solution.py:395
  111.7 1.9 %collective-permute-start.2 = (bf16[128,1024]{1,0:T(8,128)(2,1)S(1)}, bf16[128,1024]{1,0:T(8,128)(2,1)S(1)}, u32[]{:S(2)}, u32[]{:S(2)}) collective-permute-start(bf16[128,1024]{1,0:T(8,128)(2,1)S(1)} %keys_values.1.refs_0_), channel_id=1, source_target_pairs={{14,0},{15,1},{0,2},{1,3},{2,4},{3,5},{5,7},{6,8},{7,9},{8,10},{9,... | collective-permute-start | bytes 786440 | tf_op jit(solution)/shard_map/ppermute | solution.py:395
  115.0 24.7 %collective-permute-done.4.refs_4_ = bf16[128,1024]{1,0:T(8,128)(2,1)S(1)} collective-permute-done((bf16[128,1024]{1,0:T(8,128)(2,1)S(1)}, bf16[128,1024]{1,0:T(8,128)(2,1)S(1)}, u32[]{:S(2)}, u32[]{:S(2)}) %collective-permute-start.4) | collective-permute-done | bytes 262176 | tf_op jit(solution)/shard_map/ppermute | solution.py:395
  139.8 1.9 %collective-permute-start.5 = (bf16[128,1024]{1,0:T(8,128)(2,1)S(1)}, bf16[128,1024]{1,0:T(8,128)(2,1)S(1)}, u32[]{:S(2)}, u32[]{:S(2)}) collective-permute-start(bf16[128,1024]{1,0:T(8,128)(2,1)S(1)} %collective-permute-done.4.refs_4_), channel_id=1, source_target_pairs={{0,1},{1,0},{2,3},{3,2},{5,4},{9,8},{10,11},{11,10},{16,17},{17,16... | collective-permute-start | bytes 786440 | tf_op jit(solution)/shard_map/ppermute | solution.py:396
  141.7 2.7 %collective-permute-done.2.refs_2_ = bf16[128,1024]{1,0:T(8,128)(2,1)S(1)} collective-permute-done((bf16[128,1024]{1,0:T(8,128)(2,1)S(1)}, bf16[128,1024]{1,0:T(8,128)(2,1)S(1)}, u32[]{:S(2)}, u32[]{:S(2)}) %collective-permute-start.2) | collective-permute-done | bytes 262176 | tf_op jit(solution)/shard_map/ppermute | solution.py:395
  144.4 1.9 %collective-permute-start.3 = (bf16[128,1024]{1,0:T(8,128)(2,1)S(1)}, bf16[128,1024]{1,0:T(8,128)(2,1)S(1)}, u32[]{:S(2)}, u32[]{:S(2)}) collective-permute-start(bf16[128,1024]{1,0:T(8,128)(2,1)S(1)} %collective-permute-done.2.refs_2_), channel_id=1, source_target_pairs={{0,1},{1,0},{2,3},{3,2},{5,4},{7,6},{8,9},{9,8},{10,11},{11,10},{1... | collective-permute-start | bytes 786440 | tf_op jit(solution)/shard_map/ppermute | solution.py:396
  146.3 1.2 copy-done.1
  147.5 1.0 copy-done.4
  148.5 1.5 queries.1
  150.1 5.2 %attend.1 = (bf16[128,2048]{1,0:T(8,128)(2,1)}, bf16[128,2048]{1,0:T(8,128)(2,1)S(1)}) custom-call(s32[40]{0:T(128)S(1)} %copy-done.8, bf16[4,512,128]{2,1,0:T(8,128)(2,1)S(1)} %queries.1, bf16[128,1024]{1,0:T(8,128)(2,1)S(1)} %keys_values.1.refs_0_, bf16[128,1024]{1,0:T(8,128)(2,1)S(1)} %copy-done.11, bf16[128,1024]{1,0:T(8,128)(2,1)S(1)} %collective-permute-done.2.refs_2_, ...), custom_call_target="tpu_custom_call" | custom-call | flops 2000000000 | bytes 8388608 | tf_op jit(solution)/shard_map/attend/pallas_call | solution.py:321
  155.3 3.0 %output.1 = bf16[128,4096]{1,0:T(8,128)(2,1)} custom-call(bf16[128,2048]{1,0:T(8,128)(2,1)S(1)} %get-tuple-element.18.attended_ref, bf16[2,16,16,768]{3,2,1,0:T(8,128)(2,1)} %bitcast.8.piece_ref), custom_call_target="tpu_custom_call" | custom-call | flops 100000000 | bytes 3145728 | tf_op jit(solution)/shard_map/output/pallas_call | solution.py:354
  (43 shorter events, 5.9 us)
Async XLA Ops:
  0.7 1.8 %copy-start.2 = (bf16[1,64,21504]{2,1,0:T(8,128)(2,1)S(1)}, bf16[1,64,21504]{2,1,0:T(8,128)(2,1)}, u32[]{:S(2)}) copy-start(bf16[1,64,21504]{2,1,0:T(8,128)(2,1)} %bank_ref.1) | copy-start | bytes 8257540
  2.5 1.8 %copy-start.9 = (s32[2]{0:T(128)}, s32[2]{0:T(128)S(1)}, u32[]{:S(2)}) copy-start(s32[2]{0:T(128)S(1)} %pad_add_fusion.1.me_ref.x_ref) | copy-start | bytes 28
  4.3 7.5 %copy-start.12 = (s32[3]{0:T(128)S(1)}, s32[3]{0:T(128)}, u32[]{:S(2)}) copy-start(s32[3]{0:T(128)} %param.14) | copy-start | bytes 40
  4.3 7.5 %copy-start.13 = (s32[3]{0:T(128)S(1)}, s32[3]{0:T(128)}, u32[]{:S(2)}) copy-start(s32[3]{0:T(128)} %param.13) | copy-start | bytes 40
  4.3 36.1 %all-to-all-start = ((bf16[16,16,2688]{2,1,0:T(8,128)(2,1)}), bf16[16,16,2688]{2,1,0:T(8,128)(2,1)S(1)}, u32[]{:S(2)}, u32[]{:S(2)}) async-start(bf16[16,16,2688]{2,1,0:T(8,128)(2,1)} %pack.1), calls=%async_computation | async-start | bytes 2752512 | tf_op jit(solution)/shard_map/all_to_all | solution.py:427
  11.8 4.1 %collective-permute-start = (s32[2,1,3]{2,0,1:T(2,128)S(1)}, s32[2,1,3]{2,0,1:T(2,128)S(1)}, u32[]{:S(2)}, u32[]{:S(2)}) collective-permute-start(s32[2,1,3]{2,0,1:T(2,128)S(1)} %add_bitcast_fusion), channel_id=1, source_target_pairs={{0,16},{16,0},{1,17},{17,1},{2,18},{18,2},{3,19},{19,3},{4,20},{20... | collective-permute-start | bytes 80 | tf_op jit(solution)/shard_map/ppermute | solution.py:432
  41.8 0.9 copy-start.3
  42.7 54.9 %copy-start = (bf16[128,4096]{1,0:T(8,128)(2,1)S(1)}, bf16[128,4096]{1,0:T(8,128)(2,1)}, u32[]{:S(2)}) copy-start(bf16[128,4096]{1,0:T(8,128)(2,1)} %hidden_ref.3) | copy-start | bytes 3145732
  42.7 54.9 %copy-start.5 = (bf16[128,512]{1,0:T(8,128)(2,1)S(1)}, bf16[128,512]{1,0:T(8,128)(2,1)}, u32[]{:S(2)}) copy-start(bf16[128,512]{1,0:T(8,128)(2,1)} %key_ref.1) | copy-start | bytes 393220
  42.7 54.9 %copy-start.6 = (bf16[128,512]{1,0:T(8,128)(2,1)S(1)}, bf16[128,512]{1,0:T(8,128)(2,1)}, u32[]{:S(2)}) copy-start(bf16[128,512]{1,0:T(8,128)(2,1)} %value_ref.1) | copy-start | bytes 393220
  42.7 54.9 %copy-start.8 = (s32[40]{0:T(128)S(1)}, s32[40]{0:T(128)}, u32[]{:S(2)}) copy-start(s32[40]{0:T(128)} %plan.1.plan_ref) | copy-start | bytes 484
  98.8 2.7 %collective-permute-start.1 = (bf16[128,1024]{1,0:T(8,128)(2,1)S(1)}, bf16[128,1024]{1,0:T(8,128)(2,1)S(1)}, u32[]{:S(2)}, u32[]{:S(2)}) collective-permute-start(bf16[128,1024]{1,0:T(8,128)(2,1)S(1)} %keys_values.1.refs_0_), channel_id=1, source_target_pairs={{0,1},{2,3},{6,7},{8,9},{10,11},{12,13},{14,15},{16,17},{18,19},{2... | collective-permute-start | bytes 786440 | tf_op jit(solution)/shard_map/ppermute | solution.py:396
  102.2 53.1 %all-to-all-start.2 = ((bf16[32,16,768]{2,1,0:T(8,128)(2,1)}), bf16[32,16,768]{2,1,0:T(8,128)(2,1)}, u32[]{:S(2)}, u32[]{:S(2)}) async-start(bf16[32,16,768]{2,1,0:T(8,128)(2,1)} %copy-done.3), calls=%async_computation.2 | async-start | bytes 1572864 | tf_op jit(solution)/shard_map/all_to_all | solution.py:439
  105.6 8.1 %collective-permute-start.8 = (bf16[128,1024]{1,0:T(8,128)(2,1)S(1)}, bf16[128,1024]{1,0:T(8,128)(2,1)S(1)}, u32[]{:S(2)}, u32[]{:S(2)}) collective-permute-start(bf16[128,1024]{1,0:T(8,128)(2,1)S(1)} %keys_values.1.refs_0_), channel_id=1, source_target_pairs={{12,4},{13,5},{28,20},{29,21}} | collective-permute-start | bytes 786440 | tf_op jit(solution)/shard_map/ppermute | solution.py:395
  106.3 8.1 %collective-permute-start.6 = (bf16[128,1024]{1,0:T(8,128)(2,1)S(1)}, bf16[128,1024]{1,0:T(8,128)(2,1)S(1)}, u32[]{:S(2)}, u32[]{:S(2)}) collective-permute-start(bf16[128,1024]{1,0:T(8,128)(2,1)S(1)} %keys_values.1.refs_0_), channel_id=1, source_target_pairs={{12,2},{13,3},{14,4},{15,5},{5,11},{28,18},{29,19},{30,20},{31,21}... | collective-permute-start | bytes 786440 | tf_op jit(solution)/shard_map/ppermute | solution.py:395
  107.0 32.8 %collective-permute-start.4 = (bf16[128,1024]{1,0:T(8,128)(2,1)S(1)}, bf16[128,1024]{1,0:T(8,128)(2,1)S(1)}, u32[]{:S(2)}, u32[]{:S(2)}) collective-permute-start(bf16[128,1024]{1,0:T(8,128)(2,1)S(1)} %keys_values.1.refs_0_), channel_id=1, source_target_pairs={{12,0},{13,1},{14,2},{15,3},{0,4},{1,5},{5,9},{6,10},{7,11},{28,16... | collective-permute-start | bytes 786440 | tf_op jit(solution)/shard_map/ppermute | solution.py:395
  111.7 32.6 %collective-permute-start.2 = (bf16[128,1024]{1,0:T(8,128)(2,1)S(1)}, bf16[128,1024]{1,0:T(8,128)(2,1)S(1)}, u32[]{:S(2)}, u32[]{:S(2)}) collective-permute-start(bf16[128,1024]{1,0:T(8,128)(2,1)S(1)} %keys_values.1.refs_0_), channel_id=1, source_target_pairs={{14,0},{15,1},{0,2},{1,3},{2,4},{3,5},{5,7},{6,8},{7,9},{8,10},{9,... | collective-permute-start | bytes 786440 | tf_op jit(solution)/shard_map/ppermute | solution.py:395
  113.7 36.4 %collective-permute-start.9 = (bf16[128,1024]{1,0:T(8,128)(2,1)S(1)}, bf16[128,1024]{1,0:T(8,128)(2,1)S(1)}, u32[]{:S(2)}, u32[]{:S(2)}) collective-permute-start(bf16[128,1024]{1,0:T(8,128)(2,1)S(1)} %collective-permute-done.8.refs_8_), channel_id=1, source_target_pairs={{5,4},{21,20}} | collective-permute-start | bytes 786440 | tf_op jit(solution)/shard_map/ppermute | solution.py:396
  114.4 35.7 %collective-permute-start.7 = (bf16[128,1024]{1,0:T(8,128)(2,1)S(1)}, bf16[128,1024]{1,0:T(8,128)(2,1)S(1)}, u32[]{:S(2)}, u32[]{:S(2)}) collective-permute-start(bf16[128,1024]{1,0:T(8,128)(2,1)S(1)} %collective-permute-done.6.refs_6_), channel_id=1, source_target_pairs={{2,3},{3,2},{5,4},{11,10},{18,19},{19,18},{21,20},{27,26}} | collective-permute-start | bytes 786440 | tf_op jit(solution)/shard_map/ppermute | solution.py:396
  139.8 10.3 %collective-permute-start.5 = (bf16[128,1024]{1,0:T(8,128)(2,1)S(1)}, bf16[128,1024]{1,0:T(8,128)(2,1)S(1)}, u32[]{:S(2)}, u32[]{:S(2)}) collective-permute-start(bf16[128,1024]{1,0:T(8,128)(2,1)S(1)} %collective-permute-done.4.refs_4_), channel_id=1, source_target_pairs={{0,1},{1,0},{2,3},{3,2},{5,4},{9,8},{10,11},{11,10},{16,17},{17,16... | collective-permute-start | bytes 786440 | tf_op jit(solution)/shard_map/ppermute | solution.py:396
  144.4 5.7 %collective-permute-start.3 = (bf16[128,1024]{1,0:T(8,128)(2,1)S(1)}, bf16[128,1024]{1,0:T(8,128)(2,1)S(1)}, u32[]{:S(2)}, u32[]{:S(2)}) collective-permute-start(bf16[128,1024]{1,0:T(8,128)(2,1)S(1)} %collective-permute-done.2.refs_2_), channel_id=1, source_target_pairs={{0,1},{1,0},{2,3},{3,2},{5,4},{7,6},{8,9},{9,8},{10,11},{11,10},{1... | collective-permute-start | bytes 786440 | tf_op jit(solution)/shard_map/ppermute | solution.py:396
  146.3 1.2 copy-start.1
  147.5 1.0 copy-start.4
  148.5 1.6 copy-start.11
  (2 other events, 1.3 us)
